TPU v7x, 1024 devices: a whole 4x8x16 slice. The times are simulated.
1024 devices in a mesh: blk: 32 (over x_lo, z), shard: 32 (over y, x_hi, core).
Axes of the slice: x: 4 (x_hi: 2, x_lo: 2; x = x_hi * 2 + x_lo), y: 8, z: 16, core: 2. Of those that a mesh axis runs over, the one named last changes fastest.
Arguments:
- features: bfloat16 [32, 16384, 256], P('shard', 'blk'), may hold values from -6 to 6
- dense_tiles: bfloat16 [32, 32, 5, 12, 128, 128], P('shard', 'blk'), may hold values from -0.125 to 0.125
- dense_rows: int32 [32, 32, 5, 12], P('shard', 'blk'), may hold values from 0 to 3, as said below
- dense_cols: int32 [32, 32, 5, 12], P('shard', 'blk'), may hold values from 0 to 3
- send_rows: int32 [32, 32, 32, 16], P('shard', 'blk'), may hold values from 0 to 511
- sparse_target_row: int32 [32, 32, 32, 16], P('shard', 'blk'), may hold values from 0 to 511
- sparse_val: bfloat16 [32, 32, 32, 16], P('shard', 'blk'), may hold values from -4 to 4
- sparse_count: int32 [32, 32, 32], P('shard', 'blk'), may hold values from 1 to 16, as said below
- weight: bfloat16 [256, 256], replicated, may hold values from -0.375 to 0.375
Outputs:
- hidden_out: bfloat16 [32, 16384, 256], P('shard', 'blk')
Inputs may be any that keep to these rules, and one draw needn't show every extreme that they name: For each device and source block the 12 pairs (dense_rows, dense_cols) are distinct. `sparse_count`: every device has 16 live slots from the next shard index.
All inputs are finite; a program needn't handle non-finite values.
Results may differ from a plain program's by a relative error of at most 0.015.
Values may be sent and summed in bfloat16 or wider, within the bound.
A program may use at most 32 MiB of HBM per device.

v0:
```python
import jax
import jax.numpy as jnp
from jax import lax
from jax.sharding import PartitionSpec as P


def shifted(block, axis, distance):
    devices = range(lax.axis_size(axis))
    route = [((i - distance) % len(devices), i) for i in devices]
    return lax.ppermute(block, axis, route)


def local(
    features,
    dense_tiles,
    dense_rows,
    dense_cols,
    send_rows,
    sparse_target_row,
    sparse_val,
    sparse_count,
    weight,
):
    rows_dev = features.shape[1]
    feat = features.shape[2]
    tile = dense_tiles.shape[4]
    row_tiles = rows_dev // tile
    span = (dense_tiles.shape[2] - 1) // 2
    peers = send_rows.shape[2]
    slots = send_rows.shape[3]
    tiles = dense_tiles[0, 0]
    tile_rows = dense_rows[0, 0]
    tile_cols = dense_cols[0, 0]
    own = features[0]
    current_tile_index = jnp.arange(row_tiles, dtype=jnp.int32)

    def add_block(total, block_feats, which):
        pieces = block_feats.reshape(row_tiles, tile, feat)
        picked = pieces[tile_cols[which]]
        prods = jnp.einsum("tab,tbf->taf", tiles[which], picked, preferred_element_type=jnp.float32)
        onehot = (tile_rows[which][:, None] == current_tile_index[None, :]).astype(jnp.float32)
        return total + jnp.einsum("tr,taf->raf", onehot, prods)

    total = add_block(jnp.zeros((row_tiles, tile, feat), jnp.float32), own, span)
    for offset in range(-span, span + 1):
        if offset != 0:
            arrived = shifted(own, "blk", -offset)
            total = add_block(total, arrived, offset + span)
    dense_part = total.reshape(rows_dev, feat)
    outgoing = own[send_rows[0, 0]]
    received_features = lax.all_to_all(outgoing, "shard", split_axis=0, concat_axis=0, tiled=True)
    live = jnp.arange(slots, dtype=jnp.int32)[None, :] < sparse_count[0, 0][:, None]
    values = jnp.where(live, sparse_val[0, 0], jnp.zeros_like(sparse_val[0, 0]))
    placing = (sparse_target_row[0, 0][..., None] == jnp.arange(rows_dev, dtype=jnp.int32)).astype(
        jnp.bfloat16
    ) * values[..., None]
    sparse_contribution = jnp.einsum(
        "kr,kf->rf",
        placing.reshape(peers * slots, rows_dev),
        received_features.reshape(peers * slots, feat),
        preferred_element_type=jnp.float32,
    )
    gathered_messages = (dense_part + sparse_contribution).astype(jnp.bfloat16)
    product = jnp.dot(gathered_messages, weight, preferred_element_type=jnp.float32)
    return jnp.maximum(product, 0.0).astype(jnp.bfloat16)[None]


def solution(mesh):
    return jax.shard_map(
        local,
        mesh=mesh,
        in_specs=(
            P("shard", "blk", None),
            P("shard", "blk", None, None, None, None),
            P("shard", "blk", None, None),
            P("shard", "blk", None, None),
            P("shard", "blk", None, None),
            P("shard", "blk", None, None),
            P("shard", "blk", None, None),
            P("shard", "blk", None),
            P(),
        ),
        out_specs=P("shard", "blk", None),
        check_vma=False,
    )
```

profile of v0, /device:TPU:1, one launch (start us, length us, event | category | flops | bytes accessed | tf_op | source)
XLA Modules:
  0.0 76.0 jit_solution(7333152400694934899)
XLA Ops:
  0.0 19.8 %collective-permute-start.2 = (bf16[512,256]{1,0:T(8,128)(2,1)}, bf16[512,256]{1,0:T(8,128)(2,1)S(1)}, u32[]{:S(2)}, u32[]{:S(2)}) collective-permute-start(bf16[512,256]{1,0:T(8,128)(2,1)} %bitcast.116), channel_id=1, source_target_pairs={{32,0},{64,32},{96,64},{128,96},{160,128},{192,160},{224,192},{256... | collective-permute-start | bytes 786440 | tf_op jit(solution)/shard_map/ppermute | solution.py:10
  19.9 1.9 %collective-permute-start.1 = (bf16[512,256]{1,0:T(8,128)(2,1)}, bf16[512,256]{1,0:T(8,128)(2,1)}, u32[]{:S(2)}, u32[]{:S(2)}) collective-permute-start(bf16[512,256]{1,0:T(8,128)(2,1)} %bitcast.117), channel_id=1, source_target_pairs={{992,0},{0,32},{32,64},{64,96},{96,128},{128,160},{160,192},{192,2... | collective-permute-start | bytes 786440 | tf_op jit(solution)/shard_map/ppermute | solution.py:10
  21.8 1.9 %collective-permute-start = (bf16[512,256]{1,0:T(8,128)(2,1)}, bf16[512,256]{1,0:T(8,128)(2,1)S(1)}, u32[]{:S(2)}, u32[]{:S(2)}) collective-permute-start(bf16[512,256]{1,0:T(8,128)(2,1)} %bitcast.118), channel_id=1, source_target_pairs={{960,0},{992,32},{0,64},{32,96},{64,128},{96,160},{128,192},{160,2... | collective-permute-start | bytes 786440 | tf_op jit(solution)/shard_map/ppermute | solution.py:10
  23.7 6.4 %collective-permute-start.3 = (bf16[512,256]{1,0:T(8,128)(2,1)}, bf16[512,256]{1,0:T(8,128)(2,1)S(1)}, u32[]{:S(2)}, u32[]{:S(2)}) collective-permute-start(bf16[512,256]{1,0:T(8,128)(2,1)} %bitcast.119), channel_id=1, source_target_pairs={{64,0},{96,32},{128,64},{160,96},{192,128},{224,160},{256,192},{28... | collective-permute-start | bytes 786440 | tf_op jit(solution)/shard_map/ppermute | solution.py:10
  30.1 0.7 compare_select_fusion
  31.0 3.2 %gather_fusion.5 = bf16[512,256]{1,0:T(8,128)(2,1)} fusion(bf16[512,256]{1,0:T(8,128)(2,1)} %bitcast.120, s32[1024]{0:T(1024)S(1)} %pad_clamp_fusion), kind=kCustom, calls=%fused_computation.5 | custom fusion | bytes 526336 | tf_op jit(solution)/shard_map/gather | solution.py:50
  34.2 11.1 %all-to-all-start = ((bf16[32,16,256]{2,1,0:T(8,128)(2,1)}), bf16[32,16,256]{2,1,0:T(8,128)(2,1)}, u32[]{:S(2)}, u32[]{:S(2)}) async-start(bf16[32,16,256]{2,1,0:T(8,128)(2,1)} %bitcast.41), calls=%async_computation | async-start | bytes 524288 | tf_op jit(solution)/shard_map/all_to_all | solution.py:51
  45.3 0.6 pad_clamp_fusion.3
  47.1 1.4 %fusion.39 = bf16[12,256,128]{2,1,0:T(8,128)(2,1)S(1)} fusion(bf16[12,128,256]{2,1,0:T(8,128)(2,1)S(1)} %gather_fusion, bf16[1,1,5,12,128,128]{5,4,3,2,1,0:T(8,128)(2,1)} %param.10), kind=kOutput, calls=%fused_computation.37 | convolution fusion | flops 100663296 | bytes 1966080 | tf_op jit(solution)/shard_map/tab,tbf->taf/dot_general | solution.py:40
  49.2 1.0 %copy.16 = bf16[12,256,128]{1,0,2:T(8,128)(2,1)S(1)} copy(bf16[12,256,128]{2,1,0:T(8,128)(2,1)S(1)} %fusion.39) | data formatting | bytes 1572864 | tf_op jit(solution)/shard_map/tab,tbf->taf/dot_general | solution.py:40
  50.3 0.7 copy.14
  52.2 1.4 %fusion.33 = bf16[12,256,128]{2,1,0:T(8,128)(2,1)S(1)} fusion(bf16[12,128,256]{2,1,0:T(8,128)(2,1)S(1)} %gather_fusion.3, bf16[1,1,5,12,128,128]{5,4,3,2,1,0:T(8,128)(2,1)} %param.10), kind=kOutput, calls=%fused_computation.31 | convolution fusion | flops 100663296 | bytes 1966080 | tf_op jit(solution)/shard_map/tab,tbf->taf/dot_general | solution.py:40
  53.6 1.1 %copy.19 = bf16[12,256,128]{1,0,2:T(8,128)(2,1)S(1)} copy(bf16[12,256,128]{2,1,0:T(8,128)(2,1)S(1)} %fusion.33) | data formatting | bytes 1572864 | tf_op jit(solution)/shard_map/tab,tbf->taf/dot_general | solution.py:40
  54.7 2.6 %gather_fusion.2 = bf16[12,128,256]{2,1,0:T(8,128)(2,1)} fusion(bf16[4,128,256]{2,1,0:T(8,128)(2,1)} %bitcast.17, s32[1024]{0:T(1024)} %pad_clamp_fusion.3), kind=kCustom, calls=%fused_computation.2 | custom fusion | bytes 1572912 | tf_op jit(solution)/shard_map/gather | solution.py:39
  57.2 1.6 %fusion.35 = bf16[12,256,128]{2,1,0:T(8,128)(2,1)S(1)} fusion(bf16[12,128,256]{2,1,0:T(8,128)(2,1)} %gather_fusion.2, bf16[1,1,5,12,128,128]{5,4,3,2,1,0:T(8,128)(2,1)} %param.10), kind=kOutput, calls=%fused_computation.33 | convolution fusion | flops 100663296 | bytes 1966080 | tf_op jit(solution)/shard_map/tab,tbf->taf/dot_general | solution.py:40
  58.9 1.7 %copy.18 = bf16[12,256,128]{1,0,2:T(8,128)(2,1)} copy(bf16[12,256,128]{2,1,0:T(8,128)(2,1)S(1)} %fusion.35) | data formatting | bytes 1572864 | tf_op jit(solution)/shard_map/tab,tbf->taf/dot_general | solution.py:40
  60.6 1.7 %gather_fusion.1 = bf16[12,128,256]{2,1,0:T(8,128)(2,1)} fusion(bf16[4,128,256]{2,1,0:T(8,128)(2,1)S(1)} %bitcast.123, s32[1024]{0:T(1024)} %pad_clamp_fusion.4), kind=kCustom, calls=%fused_computation.1 | custom fusion | bytes 1572912 | tf_op jit(solution)/shard_map/gather | solution.py:39
  62.2 1.6 %fusion.37 = bf16[12,256,128]{2,1,0:T(8,128)(2,1)S(1)} fusion(bf16[12,128,256]{2,1,0:T(8,128)(2,1)} %gather_fusion.1, bf16[1,1,5,12,128,128]{5,4,3,2,1,0:T(8,128)(2,1)} %param.10), kind=kOutput, calls=%fused_computation.35 | convolution fusion | flops 100663296 | bytes 1966080 | tf_op jit(solution)/shard_map/tab,tbf->taf/dot_general | solution.py:40
  63.9 1.7 %copy.17 = bf16[12,256,128]{1,0,2:T(8,128)(2,1)} copy(bf16[12,256,128]{2,1,0:T(8,128)(2,1)S(1)} %fusion.37) | data formatting | bytes 1572864 | tf_op jit(solution)/shard_map/tab,tbf->taf/dot_general | solution.py:40
  65.6 0.7 gather_fusion.4
  66.3 2.3 %fusion.31 = bf16[12,256,128]{2,1,0:T(8,128)(2,1)} fusion(bf16[12,128,256]{2,1,0:T(8,128)(2,1)S(1)} %gather_fusion.4, bf16[1,1,5,12,128,128]{5,4,3,2,1,0:T(8,128)(2,1)} %param.10), kind=kOutput, calls=%fused_computation.29 | convolution fusion | flops 100663296 | bytes 1966080 | tf_op jit(solution)/shard_map/tab,tbf->taf/dot_general | solution.py:40
  68.6 2.0 %copy.20 = bf16[12,256,128]{1,0,2:T(8,128)(2,1)S(1)} copy(bf16[12,256,128]{2,1,0:T(8,128)(2,1)} %fusion.31) | data formatting | bytes 1572864 | tf_op jit(solution)/shard_map/tab,tbf->taf/dot_general | solution.py:40
  71.0 0.9 %copy-done.2 = bf16[12,256,128]{1,0,2:T(8,128)(2,1)S(1)} copy-done((bf16[12,256,128]{1,0,2:T(8,128)(2,1)S(1)}, bf16[12,256,128]{1,0,2:T(8,128)(2,1)}, u32[]{:S(2)}) %copy-start.2) | copy-done | bytes 786456
  73.6 2.4 %fusion.25 = bf16[1,512,256]{2,1,0:T(8,128)(2,1)} fusion(bf16[256,256]{1,0:T(8,128)(2,1)S(1)} %copy-done, f32[512,256]{1,0:T(8,128)S(1)} %bitcast.125, bf16[32,16,256]{2,1,0:T(8,128)(2,1)} %all-to-all-done, s32[32,16]{1,0:T(8,128)S(1)} %copy.13, bf16[32,16]{1,0:T(8,128)(2,1)S(1)} %copy-done.5), kind=kOutput, calls=%fused_computation.25 | convolution fusion | flops 202375168 | bytes 1182720 | tf_op jit(solution)/shard_map/dot_general | solution.py:64
  (53 shorter events, 5.2 us)
Async XLA Ops:
  0.0 73.5 %copy-start = (bf16[256,256]{1,0:T(8,128)(2,1)S(1)}, bf16[256,256]{1,0:T(8,128)(2,1)}, u32[]{:S(2)}) copy-start(bf16[256,256]{1,0:T(8,128)(2,1)} %param.17) | copy-start | bytes 393220
  0.0 46.5 %copy-start.1 = (bf16[1,512,256]{2,1,0:T(8,128)(2,1)S(1)}, bf16[1,512,256]{2,1,0:T(8,128)(2,1)}, u32[]{:S(2)}) copy-start(bf16[1,512,256]{2,1,0:T(8,128)(2,1)} %param.9) | copy-start | bytes 786436
  0.0 45.3 %copy-start.7 = (s32[1,1,5,12]{3,1,2,0:T(1,128)S(1)}, s32[1,1,5,12]{3,1,2,0:T(1,128)}, u32[]{:S(2)}) copy-start(s32[1,1,5,12]{3,1,2,0:T(1,128)} %param.12) | copy-start | bytes 724
  0.0 51.6 %collective-permute-start.2 = (bf16[512,256]{1,0:T(8,128)(2,1)}, bf16[512,256]{1,0:T(8,128)(2,1)S(1)}, u32[]{:S(2)}, u32[]{:S(2)}) collective-permute-start(bf16[512,256]{1,0:T(8,128)(2,1)} %bitcast.116), channel_id=1, source_target_pairs={{32,0},{64,32},{96,64},{128,96},{160,128},{192,160},{224,192},{256... | collective-permute-start | bytes 786440 | tf_op jit(solution)/shard_map/ppermute | solution.py:10
  19.9 34.8 %collective-permute-start.1 = (bf16[512,256]{1,0:T(8,128)(2,1)}, bf16[512,256]{1,0:T(8,128)(2,1)}, u32[]{:S(2)}, u32[]{:S(2)}) collective-permute-start(bf16[512,256]{1,0:T(8,128)(2,1)} %bitcast.117), channel_id=1, source_target_pairs={{992,0},{0,32},{32,64},{64,96},{96,128},{128,160},{160,192},{192,2... | collective-permute-start | bytes 786440 | tf_op jit(solution)/shard_map/ppermute | solution.py:10
  21.8 38.8 %collective-permute-start = (bf16[512,256]{1,0:T(8,128)(2,1)}, bf16[512,256]{1,0:T(8,128)(2,1)S(1)}, u32[]{:S(2)}, u32[]{:S(2)}) collective-permute-start(bf16[512,256]{1,0:T(8,128)(2,1)} %bitcast.118), channel_id=1, source_target_pairs={{960,0},{992,32},{0,64},{32,96},{64,128},{96,160},{128,192},{160,2... | collective-permute-start | bytes 786440 | tf_op jit(solution)/shard_map/ppermute | solution.py:10
  23.7 41.9 %collective-permute-start.3 = (bf16[512,256]{1,0:T(8,128)(2,1)}, bf16[512,256]{1,0:T(8,128)(2,1)S(1)}, u32[]{:S(2)}, u32[]{:S(2)}) collective-permute-start(bf16[512,256]{1,0:T(8,128)(2,1)} %bitcast.119), channel_id=1, source_target_pairs={{64,0},{96,32},{128,64},{160,96},{192,128},{224,160},{256,192},{28... | collective-permute-start | bytes 786440 | tf_op jit(solution)/shard_map/ppermute | solution.py:10
  34.1 14.4 %copy-start.6 = (bf16[1,1,32,16]{2,3,1,0:T(8,128)(2,1)S(1)}, bf16[1,1,32,16]{2,3,1,0:T(8,128)(2,1)}, u32[]{:S(2)}) copy-start(bf16[1,1,32,16]{2,3,1,0:T(8,128)(2,1)} %param.15) | copy-start | bytes 3076
  34.2 14.4 %copy-start.14 = (s32[1,1,32]{2,1,0:T(1,128)S(1)}, s32[1,1,32]{2,1,0:T(1,128)}, u32[]{:S(2)}) copy-start(s32[1,1,32]{2,1,0:T(1,128)} %param.16) | copy-start | bytes 388
  34.2 39.3 %all-to-all-start = ((bf16[32,16,256]{2,1,0:T(8,128)(2,1)}), bf16[32,16,256]{2,1,0:T(8,128)(2,1)}, u32[]{:S(2)}, u32[]{:S(2)}) async-start(bf16[32,16,256]{2,1,0:T(8,128)(2,1)} %bitcast.41), calls=%async_computation | async-start | bytes 524288 | tf_op jit(solution)/shard_map/all_to_all | solution.py:51
  47.1 3.1 %copy-start.4 = (s32[1,1,32,16]{2,3,1,0:T(8,128)S(1)}, s32[1,1,32,16]{2,3,1,0:T(8,128)}, u32[]{:S(2)}) copy-start(s32[1,1,32,16]{2,3,1,0:T(8,128)} %param.14) | copy-start | bytes 6148
  47.1 3.9 %copy-start.8 = (s32[1,1,5,12]{3,1,2,0:T(1,128)S(1)}, s32[1,1,5,12]{3,1,2,0:T(1,128)}, u32[]{:S(2)}) copy-start(s32[1,1,5,12]{3,1,2,0:T(1,128)} %param.11) | copy-start | bytes 724
  66.3 4.3 %copy-start.12 = (s32[12]{0:T(128)S(1)}, s32[12]{0:T(128)}, u32[]{:S(2)}) copy-start(s32[12]{0:T(128)} %get-tuple-element.9) | copy-start | bytes 148
  68.6 2.3 %copy-start.11 = (s32[12]{0:T(128)S(1)}, s32[12]{0:T(128)}, u32[]{:S(2)}) copy-start(s32[12]{0:T(128)} %get-tuple-element.6) | copy-start | bytes 148
  70.6 1.2 %copy-start.2 = (bf16[12,256,128]{1,0,2:T(8,128)(2,1)S(1)}, bf16[12,256,128]{1,0,2:T(8,128)(2,1)}, u32[]{:S(2)}) copy-start(bf16[12,256,128]{1,0,2:T(8,128)(2,1)} %copy.18) | copy-start | bytes 2359300
  70.6 1.5 %copy-start.3 = (bf16[12,256,128]{1,0,2:T(8,128)(2,1)S(1)}, bf16[12,256,128]{1,0,2:T(8,128)(2,1)}, u32[]{:S(2)}) copy-start(bf16[12,256,128]{1,0,2:T(8,128)(2,1)} %copy.17) | copy-start | bytes 2359300
  70.7 1.5 %copy-start.10 = (s32[12]{0:T(128)S(1)}, s32[12]{0:T(128)}, u32[]{:S(2)}) copy-start(s32[12]{0:T(128)} %get-tuple-element.7) | copy-start | bytes 148
  71.0 1.5 %copy-start.13 = (s32[12]{0:T(128)S(1)}, s32[12]{0:T(128)}, u32[]{:S(2)}) copy-start(s32[12]{0:T(128)} %get-tuple-element.8) | copy-start | bytes 148
  72.5 0.6 copy-start.9
  72.9 0.7 copy-start.5
where the time goes:
time: 76.7 us; the launch traced here: 76 us
  starting transfers between devices  41.2 us (54%)
  local copies, waits for them, and re-layouts  19.6 us (26%)
  matrix products  12.4 us (16%)
  other arithmetic  2.51 us (3%)
    ppermute x4, starting transfers between devices, shifted(): return lax.ppermute(block, axis, route)  30.1 us
    all_to_all x1, starting transfers between devices, local(): lax.all_to_all(outgoing, 'shard', split_axis=0, concat_axis=0, tiled=True)  11.1 us
    dot_general x5, matrix products, add_block(): jnp.einsum('tab,tbf->taf', tiles[which], picked, preferred_element_type=j...  8.41 us
    dot_general x5, local copies, waits for them, and re-layouts, add_block(): jnp.einsum('tab,tbf->taf', tiles[which], picked, preferred_element_type=j...  7.48 us
    gather x5, local copies, waits for them, and re-layouts, add_block(): picked = pieces[tile_cols[which]]  6.15 us
    gather x1, local copies, waits for them, and re-layouts, local(): outgoing = own[send_rows[0, 0]]  3.18 us
    dot_general x1, matrix products, local(): jnp.dot(gathered_messages, weight, preferred_element_type=jnp.float32)  2.41 us
    gather x5, other arithmetic, add_block(): picked = pieces[tile_cols[which]]  1.79 us
  transfers between devices with their start and end apart: 5, of which 0 were waited for; matrix products, arithmetic and copies ran while one was open for 41% of the time, Pallas kernels for 0%

commit v1 on v0

v1 whole, which is shorter than its diff:
```python
import functools

import jax
import jax.numpy as jnp
from jax import lax
from jax.experimental import pallas as pl
from jax.experimental.pallas import tpu as pltpu
from jax.sharding import PartitionSpec as P

MESH = pl.DeviceIdType.MESH
F32 = jnp.float32
BF16 = jnp.bfloat16


def iota(shape, axis):
    return lax.broadcasted_iota(jnp.int32, shape, axis)


def mask_of(cond, dtype):
    return jnp.where(cond, F32(1.0), F32(0.0)).astype(dtype)


def kernel(
    n_blk,
    n_shard,
    feats,
    tiles,
    t_rows,
    t_cols,
    send_rows,
    target,
    value,
    count,
    weight,
    out,
    own,
    tiles_v,
    rows_s,
    cols_s,
    send_v,
    target_v,
    value_v,
    count_v,
    weight_v,
    outgoing,
    received,
    arrived,
    acc,
    in_sem,
    tile_sem,
    blk_send,
    blk_recv,
    sh_send,
    sh_recv,
    ready,
    hello,
):
    rows_dev, feat = own.shape
    reach = tiles.shape[2]
    tpb = tiles.shape[3]
    tile = tiles.shape[4]
    span = (reach - 1) // 2
    row_tiles = rows_dev // tile
    slots, peers = send_v.shape
    lanes = peers * slots
    absent = reach * tpb
    me_b = lax.axis_index("blk")
    me_s = lax.axis_index("shard")
    right = lax.rem(me_b + 1, n_blk)
    left = lax.rem(me_b + n_blk - 1, n_blk)

    run = n_blk // 2
    hurry = lax.rem(me_b, run) >= run - 2
    quad = 4 if n_shard % 4 == 0 and n_shard > 4 else 1
    ring = n_shard // quad
    mid = ring // 2
    y, q = me_s // quad, lax.rem(me_s, quad)

    def beside(k, to=None):
        return lax.rem(y + k + ring, ring) * quad + (q if to is None else to)

    def signal(sem, shard):
        pl.semaphore_signal(sem, inc=1, device_id=(me_b, shard), device_id_type=MESH)

    def signal_row(sem, k, cond):
        @pl.when(cond)
        def _():
            for to in range(quad):
                signal(sem, beside(k, to))

    def as_int(cond):
        return jnp.where(cond, 1, 0)

    y_below, y_above = lax.rem(y + ring - 1, ring), lax.rem(y + 1, ring)
    gives_above, gives_below = y < mid, (y == 0) | (y > mid)
    has_below, has_above = y_below < mid, (y_above == 0) | (y_above > mid)
    n_after = quad * (as_int(gives_above) + as_int(gives_below))
    n_before = quad * (as_int(has_below) + as_int(has_above))

    barrier = pltpu.get_barrier_semaphore()
    pl.semaphore_signal(barrier, inc=1, device_id=(left, me_s), device_id_type=MESH)

    @pl.when(hurry)
    def _():
        signal_row(barrier, 1, gives_above)
        signal_row(barrier, -1, gives_below)

    @pl.when(jnp.logical_not(hurry))
    def _():
        def tell(k, c):
            signal(barrier, lax.rem(me_s + k, n_shard))
            return c

        lax.fori_loop(1, n_shard, tell, 0)

    pl.semaphore_wait(barrier, jnp.where(hurry, 1 + n_before, n_shard))

    def answer():
        signal_row(ready.at[0], -1, has_below)
        signal_row(ready.at[0], 1, has_above)

    def meet_near():
        pl.when(n_after > 0)(lambda: pl.semaphore_wait(ready.at[0], n_after))
        for k in (1, -1):
            signal(ready.at[1], beside(k))

    def meet_far():
        pl.semaphore_wait(ready.at[1], 2)
        known, at = 2, 2
        while known < mid:
            for k in (known, -known):
                signal(ready.at[at], beside(k))
            pl.semaphore_wait(ready.at[at], 2)
            known, at = 2 * known, at + 1

    def piece(ref, c):
        return ref.at[pl.ds(c * tile, tile)]

    def send(src, dst, way, c, to):
        copy = pltpu.make_async_remote_copy(
            src_ref=piece(src, c),
            dst_ref=piece(dst, c),
            send_sem=blk_send.at[way, c],
            recv_sem=blk_recv.at[way, c],
            device_id=(to, me_s),
            device_id_type=MESH,
        )
        copy.start()
        return copy

    first = {}
    second = {}
    for c in range(row_tiles):
        first[0, c] = send(feats.at[0], arrived.at[0], 0, c, right)
    pl.semaphore_signal(hello, inc=1, device_id=(right, me_s), device_id_type=MESH)

    def local(src, dst, sem):
        copy = pltpu.make_async_copy(src, dst, sem)
        copy.start()
        return copy

    get_own = local(feats.at[0], own, in_sem.at[0])
    get_send = local(send_rows.at[0, 0], send_v, in_sem.at[1])
    get_rows = local(t_rows.at[0], rows_s, in_sem.at[2])
    get_cols = local(t_cols.at[0], cols_s, in_sem.at[3])
    get_tiles = {
        j: local(tiles.at[0, 0, j], tiles_v.at[pl.ds(j * tpb, tpb)], tile_sem.at[j])
        for j in range(reach)
    }
    get_target = local(target.at[0, 0], target_v, in_sem.at[4])
    get_value = local(value.at[0, 0], value_v, in_sem.at[5])
    get_count = local(count.at[0], count_v, in_sem.at[6])
    get_weight = local(weight, weight_v, in_sem.at[7])

    get_send.wait()
    half = rows_dev // 2
    spread = mask_of(iota((lanes, peers), 0) // slots == iota((lanes, peers), 1), BF16)
    picks = (send_v[...] - half).astype(F32).astype(BF16)
    mine = lax.dot_general(spread, picks, (((1,), (1,)), ((), ())), preferred_element_type=F32)
    mine = jnp.where(iota((lanes, slots), 0) % slots == iota((lanes, slots), 1), mine, 0.0)
    wide = jnp.dot(mine.astype(BF16), jnp.ones((slots, 128), BF16), preferred_element_type=F32)
    pick = jnp.concatenate(
        [
            mask_of(wide == (iota((lanes, 128), 1) + (g * 128 - half)).astype(F32), BF16)
            for g in range(rows_dev // 128)
        ],
        axis=1,
    )
    get_own.wait()
    outgoing[...] = jnp.dot(pick, own[...], preferred_element_type=F32).astype(BF16)

    def give(k):
        to = lax.rem(me_s + k, n_shard)
        pltpu.make_async_remote_copy(
            src_ref=outgoing.at[pl.ds(to * slots, slots)],
            dst_ref=received.at[pl.ds(me_s * slots, slots)],
            send_sem=sh_send,
            recv_sem=sh_recv,
            device_id=(me_b, to),
            device_id_type=MESH,
        ).start()

    def exchange():
        far = n_shard // 2
        give(far)

        def both(i, c):
            give(far - i)
            give(far + i)
            return c

        lax.fori_loop(1, far, both, 0)

    pl.when(hurry)(answer)
    pl.when(jnp.logical_not(hurry))(exchange)

    pl.semaphore_wait(hello, 1)
    for c in range(row_tiles):
        first[1, c] = send(feats.at[0], arrived.at[1], 1, c, left)

    tiles_v[absent] = jnp.zeros((tile, tile), BF16)
    get_rows.wait()
    get_cols.wait()

    def block_matrix(j, cs):
        place = [rows_s[j, 0, t] * row_tiles + cols_s[j, 0, t] for t in range(tpb)]

        def pick_tile(r, c):
            at = jnp.int32(absent)
            for t in range(tpb):
                at = jnp.where(place[t] == r * row_tiles + c, j * tpb + t, at)
            return tiles_v[at]

        return jnp.concatenate(
            [
                jnp.concatenate([pick_tile(r, c) for c in cs], axis=1)
                for r in range(row_tiles)
            ],
            axis=0,
        )

    def times(j, cs, ref):
        x = ref[pl.ds(cs[0] * tile, len(cs) * tile), :]
        return jnp.dot(block_matrix(j, cs), x, preferred_element_type=F32)

    for copy in get_tiles.values():
        copy.wait()
    acc[...] = times(span, range(row_tiles), own)

    get_weight.wait()
    get_target.wait()
    get_value.wait()
    get_count.wait()
    spread_l = mask_of(iota((peers, lanes), 1) // slots == iota((peers, lanes), 0), BF16)
    slot_l = iota((slots, lanes), 1) % slots
    own_slot = slot_l == iota((slots, lanes), 0)

    def along(x):
        wide_x = jnp.dot(x, spread_l, preferred_element_type=F32)
        return jnp.sum(jnp.where(own_slot, wide_x, 0.0), axis=0, keepdims=True)

    target_l = along((target_v[...] - half).astype(F32).astype(BF16))
    value_l = along(value_v[...])
    count_l = jnp.dot(count_v[...].astype(F32).astype(BF16), spread_l, preferred_element_type=F32)
    live = (iota((1, lanes), 1) % slots).astype(F32) < count_l
    value_l = jnp.where(live, value_l, 0.0)
    placing = jnp.where(
        (iota((rows_dev, lanes), 0) - half).astype(F32) == target_l, value_l, 0.0
    ).astype(BF16)

    every = range(row_tiles)
    for c in every:
        first[0, c].wait_recv()
        second[0, c] = send(arrived.at[0], arrived.at[2], 2, c, right)
        first[1, c].wait_recv()
        second[1, c] = send(arrived.at[1], arrived.at[3], 3, c, left)
        if c == row_tiles - 2:
            pl.when(hurry)(meet_near)

    @pl.when(hurry)
    def _():
        meet_far()
        exchange()

    received[pl.ds(me_s * slots, slots), :] = outgoing[pl.ds(me_s * slots, slots), :]
    acc[...] += times(span - 1, every, arrived.at[0])
    acc[...] += times(span + 1, every, arrived.at[1])

    some = pl.ds(0, (n_shard - 1) * slots)
    pltpu.make_async_copy(received.at[some], received.at[some], sh_recv).wait()
    acc[...] += jnp.dot(placing, received[...], preferred_element_type=F32)
    for c in every:
        second[1, c].wait_recv()
    acc[...] += times(span + 2, every, arrived.at[3])

    for c in every:
        second[0, c].wait_recv()
        acc[...] += times(span - 2, [c], arrived.at[2])

    total = acc[...].astype(BF16)
    product = jnp.dot(total, weight_v[...], preferred_element_type=F32)
    out[0] = jnp.maximum(product, 0.0).astype(BF16)

    for copy in list(first.values()) + list(second.values()):
        copy.wait_send()
    pltpu.make_async_copy(outgoing.at[some], outgoing.at[some], sh_send).wait()


def layer(mesh, features, tiles, t_rows, t_cols, send_rows, target, value, count, weight):
    n_blk, n_shard = mesh.shape["blk"], mesh.shape["shard"]
    _, rows_dev, feat = features.shape
    _, _, reach, tpb, tile, _ = tiles.shape
    assert reach == 5 and rows_dev <= 512 and rows_dev % tile == 0
    _, _, peers, slots = send_rows.shape
    row_tiles = rows_dev // tile
    lanes = peers * slots
    dma = pltpu.SemaphoreType.DMA
    flops = 2 * feat * (reach * rows_dev * rows_dev + 2 * rows_dev * lanes + rows_dev * feat)
    return pl.pallas_call(
        functools.partial(kernel, n_blk, n_shard),
        out_shape=pltpu.VMEM((1, rows_dev, feat), BF16),
        in_specs=[pl.BlockSpec(memory_space=pl.ANY)] * 9,
        out_specs=pl.BlockSpec(memory_space=pltpu.VMEM),
        scratch_shapes=[
            pltpu.VMEM((rows_dev, feat), BF16),
            pltpu.VMEM((reach * tpb + 1, tile, tile), BF16),
            pltpu.SMEM((reach, 1, tpb), jnp.int32),
            pltpu.SMEM((reach, 1, tpb), jnp.int32),
            pltpu.VMEM((slots, peers), jnp.int32),
            pltpu.VMEM((slots, peers), jnp.int32),
            pltpu.VMEM((slots, peers), BF16),
            pltpu.VMEM((1, peers), jnp.int32),
            pltpu.VMEM((feat, feat), BF16),
            pltpu.VMEM((lanes, feat), BF16),
            pltpu.VMEM((lanes, feat), BF16),
            pltpu.VMEM((4, rows_dev, feat), BF16),
            pltpu.VMEM((rows_dev, feat), F32),
            dma((8,)),
            dma((reach,)),
            dma((4, row_tiles)),
            dma((4, row_tiles)),
            dma,
            dma,
            pltpu.SemaphoreType.REGULAR((8,)),
            pltpu.SemaphoreType.REGULAR,
        ],
        compiler_params=pltpu.CompilerParams(
            collective_id=0, has_side_effects=True, vmem_limit_bytes=60 * 1024 * 1024
        ),
        cost_estimate=pl.CostEstimate(flops=flops, bytes_accessed=4 << 20, transcendentals=0),
    )(
        features,
        tiles,
        t_rows.transpose(0, 2, 1, 3),
        t_cols.transpose(0, 2, 1, 3),
        send_rows.transpose(0, 1, 3, 2),
        target.transpose(0, 1, 3, 2),
        value.transpose(0, 1, 3, 2),
        count,
        weight,
    )


def solution(mesh):
    return jax.shard_map(
        functools.partial(layer, mesh),
        mesh=mesh,
        in_specs=(
            P("shard", "blk", None),
            P("shard", "blk", None, None, None, None),
            P("shard", "blk", None, None),
            P("shard", "blk", None, None),
            P("shard", "blk", None, None),
            P("shard", "blk", None, None),
            P("shard", "blk", None, None),
            P("shard", "blk", None),
            P(),
        ),
        out_specs=P("shard", "blk", None),
        check_vma=False,
    )
```

time: 76.7 us -> 35.7 us (0.47)
  the two profiles are of different devices: /device:TPU:1 before, /device:TPU:10 now
where the time goes in v1:
time: 35.7 us; the launch traced here: 35.6 us
  Pallas kernels  34.9 us (98%)
  local copies, waits for them, and re-layouts  0.71 us (2%)
    pallas_call x1, Pallas kernels, layer(): pl.pallas_call(functools.partial(kernel, n_blk, n_shard), out_shape=pltpu...  34.9 us

profile of v1, /device:TPU:10, one launch (start us, length us, event | category | flops | bytes accessed | tf_op | source)
XLA Modules:
  0.0 35.6 jit_solution(15549300116418436530)
XLA Ops:
  0.0 34.9 %shard_map.91 = bf16[1,512,256]{2,1,0:T(8,128)(2,1)S(1)} custom-call(bf16[1,512,256]{2,1,0:T(8,128)(2,1)} %feats.1, bf16[1,1,5,12,128,128]{5,4,3,2,1,0:T(8,128)(2,1)} %tiles.1, s32[1,5,1,12]{3,2,1,0:T(1,128)} %bitcast.8, s32[1,5,1,12]{3,2,1,0:T(1,128)} %bitcast.9, s32[1,1,16,32]{3,2,1,0:T(8,128)} %bitcast.5, s32[1,1,16,32]{3,2,1,0:T(8,128)} %bitcast.6, ...), custom_call_target="tpu_custom_call" | custom-call | flops 1006632960 | bytes 4194304 | tf_op jit(solution)/shard_map/pallas_call | solution.py:319
  34.9 0.7 %copy.11 = bf16[1,512,256]{2,1,0:T(8,128)(2,1)} copy(bf16[1,512,256]{2,1,0:T(8,128)(2,1)S(1)} %shard_map.91) | data formatting | bytes 524288

commit v2 on v1

--- a/solution.py
+++ b/solution.py
@@ -70,7 +70,10 @@
     left = lax.rem(me_b + n_blk - 1, n_blk)
 
     run = n_blk // 2
-    hurry = lax.rem(me_b, run) >= run - 2
+    left3 = lax.rem(me_b + n_blk - 3, n_blk)
+    z = lax.rem(me_b, run)
+    is_first, is_second, is_third, is_last, by_row = z == 0, z == 1, z == 2, z == run - 1, z == run - 2
+    direct = z < run - 2
     quad = 4 if n_shard % 4 == 0 and n_shard > 4 else 1
     ring = n_shard // quad
     mid = ring // 2
@@ -100,20 +103,24 @@
     barrier = pltpu.get_barrier_semaphore()
     pl.semaphore_signal(barrier, inc=1, device_id=(left, me_s), device_id_type=MESH)
 
-    @pl.when(hurry)
+    @pl.when(by_row)
     def _():
         signal_row(barrier, 1, gives_above)
         signal_row(barrier, -1, gives_below)
 
-    @pl.when(jnp.logical_not(hurry))
-    def _():
+    def tell_all(sem):
         def tell(k, c):
-            signal(barrier, lax.rem(me_s + k, n_shard))
+            signal(sem, lax.rem(me_s + k, n_shard))
             return c
 
         lax.fori_loop(1, n_shard, tell, 0)
 
-    pl.semaphore_wait(barrier, jnp.where(hurry, 1 + n_before, n_shard))
+    straggler = (me_b == 0) & (me_s == 0)
+    without = (me_b == 0) & (me_s != 0)
+    pl.when(direct & jnp.logical_not(straggler))(lambda: tell_all(barrier))
+    needed = jnp.where(without, n_shard - 1, n_shard)
+    pl.semaphore_wait(barrier, jnp.where(direct, needed, jnp.where(by_row, 1 + n_before, 1)))
+    pl.when(straggler)(lambda: tell_all(ready.at[4]))
 
     def answer():
         signal_row(ready.at[0], -1, has_below)
@@ -136,15 +143,18 @@
     def piece(ref, c):
         return ref.at[pl.ds(c * tile, tile)]
 
-    def send(src, dst, way, c, to):
-        copy = pltpu.make_async_remote_copy(
+    def pieces(src, dst, way, sent, c, to):
+        return pltpu.make_async_remote_copy(
             src_ref=piece(src, c),
             dst_ref=piece(dst, c),
-            send_sem=blk_send.at[way, c],
+            send_sem=blk_send.at[sent, c],
             recv_sem=blk_recv.at[way, c],
             device_id=(to, me_s),
             device_id_type=MESH,
         )
+
+    def send(src, dst, way, c, to):
+        copy = pieces(src, dst, way, way, c, to)
         copy.start()
         return copy
 
@@ -172,22 +182,22 @@
     get_count = local(count.at[0], count_v, in_sem.at[6])
     get_weight = local(weight, weight_v, in_sem.at[7])
 
-    get_send.wait()
     half = rows_dev // 2
-    spread = mask_of(iota((lanes, peers), 0) // slots == iota((lanes, peers), 1), BF16)
-    picks = (send_v[...] - half).astype(F32).astype(BF16)
-    mine = lax.dot_general(spread, picks, (((1,), (1,)), ((), ())), preferred_element_type=F32)
-    mine = jnp.where(iota((lanes, slots), 0) % slots == iota((lanes, slots), 1), mine, 0.0)
-    wide = jnp.dot(mine.astype(BF16), jnp.ones((slots, 128), BF16), preferred_element_type=F32)
-    pick = jnp.concatenate(
-        [
-            mask_of(wide == (iota((lanes, 128), 1) + (g * 128 - half)).astype(F32), BF16)
-            for g in range(rows_dev // 128)
-        ],
-        axis=1,
-    )
-    get_own.wait()
-    outgoing[...] = jnp.dot(pick, own[...], preferred_element_type=F32).astype(BF16)
+
+    def gather():
+        spread = mask_of(iota((lanes, peers), 0) // slots == iota((lanes, peers), 1), BF16)
+        picks = (send_v[...] - half).astype(F32).astype(BF16)
+        mine = lax.dot_general(spread, picks, (((1,), (1,)), ((), ())), preferred_element_type=F32)
+        mine = jnp.where(iota((lanes, slots), 0) % slots == iota((lanes, slots), 1), mine, 0.0)
+        wide = jnp.dot(mine.astype(BF16), jnp.ones((slots, 128), BF16), preferred_element_type=F32)
+        pick = jnp.concatenate(
+            [
+                mask_of(wide == (iota((lanes, 128), 1) + (g * 128 - half)).astype(F32), BF16)
+                for g in range(rows_dev // 128)
+            ],
+            axis=1,
+        )
+        outgoing[...] = jnp.dot(pick, own[...], preferred_element_type=F32).astype(BF16)
 
     def give(k):
         to = lax.rem(me_s + k, n_shard)
@@ -201,22 +211,65 @@
         ).start()
 
     def exchange():
+        gather()
         far = n_shard // 2
-        give(far)
+
+        def but(k):
+            skip = without & (lax.rem(me_s + k, n_shard) == 0)
+            pl.when(jnp.logical_not(skip))(lambda: give(k))
+
+        but(far)
 
         def both(i, c):
-            give(far - i)
-            give(far + i)
+            but(far - i)
+            but(far + i)
             return c
 
         lax.fori_loop(1, far, both, 0)
 
-    pl.when(hurry)(answer)
-    pl.when(jnp.logical_not(hurry))(exchange)
+    pl.when(by_row)(answer)
+    get_send.wait()
+    get_own.wait()
+    pl.when(direct)(exchange)
 
     pl.semaphore_wait(hello, 1)
+
+    @pl.when(without)
+    def _():
+        pl.semaphore_wait(ready.at[4], 1)
+        give(n_shard - me_s)
+
     for c in range(row_tiles):
         first[1, c] = send(feats.at[0], arrived.at[1], 1, c, left)
+    pl.when(is_first)(lambda: tell_all(ready.at[6]))
+
+    every = range(row_tiles)
+    for c in every:
+        first[0, c].wait_recv()
+        second[0, c] = send(arrived.at[0], arrived.at[2], 2, c, right)
+        first[1, c].wait_recv()
+        second[1, c] = pieces(arrived.at[1], arrived.at[3], 3, 3, c, left)
+        pl.when(jnp.logical_not(is_first))(second[1, c].start)
+        if c == row_tiles - 2:
+            pl.when(by_row)(meet_near)
+
+    third = [pieces(arrived.at[0], arrived.at[3], 3, 4, c, left3) for c in every]
+
+    @pl.when(is_third)
+    def _():
+        pl.semaphore_wait(ready.at[5], 1)
+        for copy in third:
+            copy.start()
+
+    @pl.when(by_row)
+    def _():
+        meet_far()
+        exchange()
+
+    @pl.when(is_last)
+    def _():
+        pl.semaphore_wait(ready.at[7], 1)
+        exchange()
 
     tiles_v[absent] = jnp.zeros((tile, tile), BF16)
     get_rows.wait()
@@ -268,20 +321,6 @@
         (iota((rows_dev, lanes), 0) - half).astype(F32) == target_l, value_l, 0.0
     ).astype(BF16)
 
-    every = range(row_tiles)
-    for c in every:
-        first[0, c].wait_recv()
-        second[0, c] = send(arrived.at[0], arrived.at[2], 2, c, right)
-        first[1, c].wait_recv()
-        second[1, c] = send(arrived.at[1], arrived.at[3], 3, c, left)
-        if c == row_tiles - 2:
-            pl.when(hurry)(meet_near)
-
-    @pl.when(hurry)
-    def _():
-        meet_far()
-        exchange()
-
     received[pl.ds(me_s * slots, slots), :] = outgoing[pl.ds(me_s * slots, slots), :]
     acc[...] += times(span - 1, every, arrived.at[0])
     acc[...] += times(span + 1, every, arrived.at[1])
@@ -295,14 +334,35 @@
 
     for c in every:
         second[0, c].wait_recv()
+        if c == 0:
+            @pl.when(is_second)
+            def _():
+                pl.semaphore_signal(ready.at[5], inc=1, device_id=(right, me_s), device_id_type=MESH)
+
+        if c == row_tiles - 2:
+            @pl.when(is_first)
+            def _():
+                pl.semaphore_wait(ready.at[6], n_shard - 1)
+                pl.semaphore_signal(ready.at[7], inc=1, device_id=(left, me_s), device_id_type=MESH)
         acc[...] += times(span - 2, [c], arrived.at[2])
 
     total = acc[...].astype(BF16)
     product = jnp.dot(total, weight_v[...], preferred_element_type=F32)
     out[0] = jnp.maximum(product, 0.0).astype(BF16)
 
-    for copy in list(first.values()) + list(second.values()):
+    for copy in list(first.values()) + [second[0, c] for c in every]:
         copy.wait_send()
+
+    @pl.when(jnp.logical_not(is_first))
+    def _():
+        for c in every:
+            second[1, c].wait_send()
+
+    @pl.when(is_third)
+    def _():
+        for copy in third:
+            copy.wait_send()
+
     pltpu.make_async_copy(outgoing.at[some], outgoing.at[some], sh_send).wait()
 
 
@@ -337,7 +397,7 @@
             pltpu.VMEM((rows_dev, feat), F32),
             dma((8,)),
             dma((reach,)),
-            dma((4, row_tiles)),
+            dma((5, row_tiles)),
             dma((4, row_tiles)),
             dma,
             dma,

time: 35.7 us -> 32.8 us (0.919)
  the two profiles are of different devices: /device:TPU:10 before, /device:TPU:6 now
where the time goes in v2:
time: 32.8 us; the launch traced here: 32.5 us
  Pallas kernels  31.8 us (97%)
  local copies, waits for them, and re-layouts  0.71 us (2%)
    pallas_call x1, Pallas kernels, layer(): pl.pallas_call(functools.partial(kernel, n_blk, n_shard), out_shape=pltpu...  31.8 us
    unnamed x1, local copies, waits for them, and re-layouts  0.71 us

profile of v2, /device:TPU:6, one launch (start us, length us, event | category | flops | bytes accessed | tf_op | source)
XLA Modules:
  0.0 32.5 jit_solution(12812473817901742035)
XLA Ops:
  0.0 31.8 %shard_map.91 = bf16[1,512,256]{2,1,0:T(8,128)(2,1)S(1)} custom-call(bf16[1,512,256]{2,1,0:T(8,128)(2,1)} %feats.1, bf16[1,1,5,12,128,128]{5,4,3,2,1,0:T(8,128)(2,1)} %tiles.1, s32[1,5,1,12]{3,2,1,0:T(1,128)} %bitcast.8, s32[1,5,1,12]{3,2,1,0:T(1,128)} %bitcast.9, s32[1,1,16,32]{3,2,1,0:T(8,128)} %bitcast.5, s32[1,1,16,32]{3,2,1,0:T(8,128)} %bitcast.6, ...), custom_call_target="tpu_custom_call" | custom-call | flops 1006632960 | bytes 4194304 | tf_op jit(solution)/shard_map/pallas_call | solution.py:379
  31.8 0.7 %copy.11 = bf16[1,512,256]{2,1,0:T(8,128)(2,1)} copy(bf16[1,512,256]{2,1,0:T(8,128)(2,1)S(1)} %shard_map.91) | data formatting | bytes 524288

commit v3 on v2

--- a/solution.py
+++ b/solution.py
@@ -72,41 +72,14 @@
     run = n_blk // 2
     left3 = lax.rem(me_b + n_blk - 3, n_blk)
     z = lax.rem(me_b, run)
-    is_first, is_second, is_third, is_last, by_row = z == 0, z == 1, z == 2, z == run - 1, z == run - 2
+    is_first, is_second, is_third, is_last, is_late = z == 0, z == 1, z == 2, z == run - 1, z == run - 2
     direct = z < run - 2
-    quad = 4 if n_shard % 4 == 0 and n_shard > 4 else 1
-    ring = n_shard // quad
-    mid = ring // 2
-    y, q = me_s // quad, lax.rem(me_s, quad)
-
-    def beside(k, to=None):
-        return lax.rem(y + k + ring, ring) * quad + (q if to is None else to)
-
+    before_late = z == run - 3
     def signal(sem, shard):
         pl.semaphore_signal(sem, inc=1, device_id=(me_b, shard), device_id_type=MESH)
 
-    def signal_row(sem, k, cond):
-        @pl.when(cond)
-        def _():
-            for to in range(quad):
-                signal(sem, beside(k, to))
-
-    def as_int(cond):
-        return jnp.where(cond, 1, 0)
-
-    y_below, y_above = lax.rem(y + ring - 1, ring), lax.rem(y + 1, ring)
-    gives_above, gives_below = y < mid, (y == 0) | (y > mid)
-    has_below, has_above = y_below < mid, (y_above == 0) | (y_above > mid)
-    n_after = quad * (as_int(gives_above) + as_int(gives_below))
-    n_before = quad * (as_int(has_below) + as_int(has_above))
-
     barrier = pltpu.get_barrier_semaphore()
     pl.semaphore_signal(barrier, inc=1, device_id=(left, me_s), device_id_type=MESH)
-
-    @pl.when(by_row)
-    def _():
-        signal_row(barrier, 1, gives_above)
-        signal_row(barrier, -1, gives_below)
 
     def tell_all(sem):
         def tell(k, c):
@@ -119,26 +92,10 @@
     without = (me_b == 0) & (me_s != 0)
     pl.when(direct & jnp.logical_not(straggler))(lambda: tell_all(barrier))
     needed = jnp.where(without, n_shard - 1, n_shard)
-    pl.semaphore_wait(barrier, jnp.where(direct, needed, jnp.where(by_row, 1 + n_before, 1)))
-    pl.when(straggler)(lambda: tell_all(ready.at[4]))
-
-    def answer():
-        signal_row(ready.at[0], -1, has_below)
-        signal_row(ready.at[0], 1, has_above)
-
-    def meet_near():
-        pl.when(n_after > 0)(lambda: pl.semaphore_wait(ready.at[0], n_after))
-        for k in (1, -1):
-            signal(ready.at[1], beside(k))
-
-    def meet_far():
-        pl.semaphore_wait(ready.at[1], 2)
-        known, at = 2, 2
-        while known < mid:
-            for k in (known, -known):
-                signal(ready.at[at], beside(k))
-            pl.semaphore_wait(ready.at[at], 2)
-            known, at = 2 * known, at + 1
+    pl.semaphore_wait(barrier, jnp.where(direct, needed, 1))
+    pl.when(straggler)(lambda: tell_all(ready.at[3]))
+
+    pl.when(before_late)(lambda: tell_all(ready.at[0]))
 
     def piece(ref, c):
         return ref.at[pl.ds(c * tile, tile)]
@@ -162,7 +119,8 @@
     second = {}
     for c in range(row_tiles):
         first[0, c] = send(feats.at[0], arrived.at[0], 0, c, right)
-    pl.semaphore_signal(hello, inc=1, device_id=(right, me_s), device_id_type=MESH)
+        if c == 0:
+            pl.semaphore_signal(hello, inc=1, device_id=(right, me_s), device_id_type=MESH)
 
     def local(src, dst, sem):
         copy = pltpu.make_async_copy(src, dst, sem)
@@ -227,7 +185,6 @@
 
         lax.fori_loop(1, far, both, 0)
 
-    pl.when(by_row)(answer)
     get_send.wait()
     get_own.wait()
     pl.when(direct)(exchange)
@@ -236,12 +193,13 @@
 
     @pl.when(without)
     def _():
-        pl.semaphore_wait(ready.at[4], 1)
+        pl.semaphore_wait(ready.at[3], 1)
         give(n_shard - me_s)
+
+    pl.when(is_first)(lambda: tell_all(ready.at[1]))
 
     for c in range(row_tiles):
         first[1, c] = send(feats.at[0], arrived.at[1], 1, c, left)
-    pl.when(is_first)(lambda: tell_all(ready.at[6]))
 
     every = range(row_tiles)
     for c in every:
@@ -250,25 +208,28 @@
         first[1, c].wait_recv()
         second[1, c] = pieces(arrived.at[1], arrived.at[3], 3, 3, c, left)
         pl.when(jnp.logical_not(is_first))(second[1, c].start)
-        if c == row_tiles - 2:
-            pl.when(by_row)(meet_near)
 
     third = [pieces(arrived.at[0], arrived.at[3], 3, 4, c, left3) for c in every]
 
+    @pl.when(is_second)
+    def _():
+        second[0, 0].wait_recv()
+        pl.semaphore_signal(ready.at[4], inc=1, device_id=(right, me_s), device_id_type=MESH)
+
     @pl.when(is_third)
     def _():
-        pl.semaphore_wait(ready.at[5], 1)
+        pl.semaphore_wait(ready.at[4], 1)
         for copy in third:
             copy.start()
 
-    @pl.when(by_row)
-    def _():
-        meet_far()
-        exchange()
-
-    @pl.when(is_last)
-    def _():
-        pl.semaphore_wait(ready.at[7], 1)
+    @pl.when(before_late)
+    def _():
+        pl.semaphore_wait(ready.at[0], n_shard - 1)
+        pl.semaphore_signal(ready.at[2], inc=1, device_id=(right, me_s), device_id_type=MESH)
+
+    @pl.when(is_late | is_last)
+    def _():
+        pl.semaphore_wait(ready.at[2], 1)
         exchange()
 
     tiles_v[absent] = jnp.zeros((tile, tile), BF16)
@@ -333,17 +294,15 @@
     acc[...] += times(span + 2, every, arrived.at[3])
 
     for c in every:
-        second[0, c].wait_recv()
         if c == 0:
-            @pl.when(is_second)
-            def _():
-                pl.semaphore_signal(ready.at[5], inc=1, device_id=(right, me_s), device_id_type=MESH)
-
+            pl.when(jnp.logical_not(is_second))(second[0, c].wait_recv)
+        else:
+            second[0, c].wait_recv()
         if c == row_tiles - 2:
             @pl.when(is_first)
             def _():
-                pl.semaphore_wait(ready.at[6], n_shard - 1)
-                pl.semaphore_signal(ready.at[7], inc=1, device_id=(left, me_s), device_id_type=MESH)
+                pl.semaphore_wait(ready.at[1], n_shard - 1)
+                pl.semaphore_signal(ready.at[2], inc=1, device_id=(left, me_s), device_id_type=MESH)
         acc[...] += times(span - 2, [c], arrived.at[2])
 
     total = acc[...].astype(BF16)
@@ -401,7 +360,7 @@
             dma((4, row_tiles)),
             dma,
             dma,
-            pltpu.SemaphoreType.REGULAR((8,)),
+            pltpu.SemaphoreType.REGULAR((5,)),
             pltpu.SemaphoreType.REGULAR,
         ],
         compiler_params=pltpu.CompilerParams(

time: 32.8 us -> 32.6 us (level)
  no operation moved by 1% of the time
where the time goes in v3:
time: 32.6 us; the launch traced here: 32.5 us
  Pallas kernels  31.7 us (97%)
  local copies, waits for them, and re-layouts  0.71 us (2%)
    pallas_call x1, Pallas kernels, layer(): pl.pallas_call(functools.partial(kernel, n_blk, n_shard), out_shape=pltpu...  31.7 us
    unnamed x1, local copies, waits for them, and re-layouts  0.71 us

profile of v3, /device:TPU:6, one launch (start us, length us, event | category | flops | bytes accessed | tf_op | source)
XLA Modules:
  0.0 32.5 jit_solution(10582395143211898303)
XLA Ops:
  0.0 31.7 %shard_map.91 = bf16[1,512,256]{2,1,0:T(8,128)(2,1)S(1)} custom-call(bf16[1,512,256]{2,1,0:T(8,128)(2,1)} %feats.1, bf16[1,1,5,12,128,128]{5,4,3,2,1,0:T(8,128)(2,1)} %tiles.1, s32[1,5,1,12]{3,2,1,0:T(1,128)} %bitcast.8, s32[1,5,1,12]{3,2,1,0:T(1,128)} %bitcast.9, s32[1,1,16,32]{3,2,1,0:T(8,128)} %bitcast.5, s32[1,1,16,32]{3,2,1,0:T(8,128)} %bitcast.6, ...), custom_call_target="tpu_custom_call" | custom-call | flops 1006632960 | bytes 4194304 | tf_op jit(solution)/shard_map/pallas_call | solution.py:338
  31.8 0.7 %copy.11 = bf16[1,512,256]{2,1,0:T(8,128)(2,1)} copy(bf16[1,512,256]{2,1,0:T(8,128)(2,1)S(1)} %shard_map.91) | data formatting | bytes 524288

commit v4 on v3

--- a/solution.py
+++ b/solution.py
@@ -189,12 +189,12 @@
     get_own.wait()
     pl.when(direct)(exchange)
 
-    pl.semaphore_wait(hello, 1)
-
     @pl.when(without)
     def _():
         pl.semaphore_wait(ready.at[3], 1)
         give(n_shard - me_s)
+
+    pl.semaphore_wait(hello, 1)
 
     pl.when(is_first)(lambda: tell_all(ready.at[1]))
 

time: 32.6 us -> 32.2 us (0.988)
    pallas_call x1, Pallas kernels: 31.7 us -> 31.4 us  [layer(): pl.pallas_call(functools.partial(kernel, n_blk, n_shard), out_shape=pltpu...]
where the time goes in v4:
time: 32.2 us; the launch traced here: 32.1 us
  Pallas kernels  31.4 us (98%)
  local copies, waits for them, and re-layouts  0.71 us (2%)
    pallas_call x1, Pallas kernels, layer(): pl.pallas_call(functools.partial(kernel, n_blk, n_shard), out_shape=pltpu...  31.4 us
    unnamed x1, local copies, waits for them, and re-layouts  0.71 us

profile of v4, /device:TPU:6, one launch (start us, length us, event | category | flops | bytes accessed | tf_op | source)
XLA Modules:
  0.0 32.1 jit_solution(5075180298743370678)
XLA Ops:
  0.0 31.4 %shard_map.91 = bf16[1,512,256]{2,1,0:T(8,128)(2,1)S(1)} custom-call(bf16[1,512,256]{2,1,0:T(8,128)(2,1)} %feats.1, bf16[1,1,5,12,128,128]{5,4,3,2,1,0:T(8,128)(2,1)} %tiles.1, s32[1,5,1,12]{3,2,1,0:T(1,128)} %bitcast.8, s32[1,5,1,12]{3,2,1,0:T(1,128)} %bitcast.9, s32[1,1,16,32]{3,2,1,0:T(8,128)} %bitcast.5, s32[1,1,16,32]{3,2,1,0:T(8,128)} %bitcast.6, ...), custom_call_target="tpu_custom_call" | custom-call | flops 1006632960 | bytes 4194304 | tf_op jit(solution)/shard_map/pallas_call | solution.py:338
  31.4 0.7 %copy.11 = bf16[1,512,256]{2,1,0:T(8,128)(2,1)} copy(bf16[1,512,256]{2,1,0:T(8,128)(2,1)S(1)} %shard_map.91) | data formatting | bytes 524288

commit v5 on v4

--- a/solution.py
+++ b/solution.py
@@ -205,6 +205,7 @@
     for c in every:
         first[0, c].wait_recv()
         second[0, c] = send(arrived.at[0], arrived.at[2], 2, c, right)
+    for c in every:
         first[1, c].wait_recv()
         second[1, c] = pieces(arrived.at[1], arrived.at[3], 3, 3, c, left)
         pl.when(jnp.logical_not(is_first))(second[1, c].start)

time: 32.2 us -> 32.2 us (level)
  no operation moved by 1% of the time
where the time goes in v5:
time: 32.2 us; the launch traced here: 32.1 us
  Pallas kernels  31.4 us (98%)
  local copies, waits for them, and re-layouts  0.71 us (2%)
    pallas_call x1, Pallas kernels, layer(): pl.pallas_call(functools.partial(kernel, n_blk, n_shard), out_shape=pltpu...  31.4 us
    unnamed x1, local copies, waits for them, and re-layouts  0.71 us

profile of v5, /device:TPU:6, one launch (start us, length us, event | category | flops | bytes accessed | tf_op | source)
XLA Modules:
  0.0 32.1 jit_solution(16482669195440948551)
XLA Ops:
  0.0 31.4 %shard_map.91 = bf16[1,512,256]{2,1,0:T(8,128)(2,1)S(1)} custom-call(bf16[1,512,256]{2,1,0:T(8,128)(2,1)} %feats.1, bf16[1,1,5,12,128,128]{5,4,3,2,1,0:T(8,128)(2,1)} %tiles.1, s32[1,5,1,12]{3,2,1,0:T(1,128)} %bitcast.8, s32[1,5,1,12]{3,2,1,0:T(1,128)} %bitcast.9, s32[1,1,16,32]{3,2,1,0:T(8,128)} %bitcast.5, s32[1,1,16,32]{3,2,1,0:T(8,128)} %bitcast.6, ...), custom_call_target="tpu_custom_call" | custom-call | flops 1006632960 | bytes 4194304 | tf_op jit(solution)/shard_map/pallas_call | solution.py:339
  31.4 0.7 %copy.11 = bf16[1,512,256]{2,1,0:T(8,128)(2,1)} copy(bf16[1,512,256]{2,1,0:T(8,128)(2,1)S(1)} %shard_map.91) | data formatting | bytes 524288
